TPU v7x, 32 devices: a whole 2x2x4 slice. The times are simulated.
32 devices in a mesh: gx: 4 (over z), gy: 4 (over y, core), gz: 2 (over x).
Axes of the slice: x: 2, y: 2, z: 4, core: 2. Of those that a mesh axis runs over, the one named last changes fastest.
Arguments:
- rhs: float32 [128, 128, 256], P('gx', 'gy', 'gz'), may hold values from -8 to 8
- accumulation: float32 [128, 128, 256], P('gx', 'gy', 'gz'), may hold values from 0.05 to 0.5
- permeability: float32 [3, 128, 128, 256], P(None, 'gx', 'gy', 'gz'), may hold values from 0.1 to 10
- nnc_cell: int32 [4, 4, 2, 512], P('gx', 'gy', 'gz'), may hold values from 0 to 4095, as said below
- nnc_remote: int32 [4, 4, 2, 512], P('gx', 'gy', 'gz'), may hold values from 0 to 8191, as said below
- nnc_mask: int32 [4, 4, 2, 512], P('gx', 'gy', 'gz'), may hold values from 0 to 1, as said below
- nnc_trans: float32 [4, 4, 2, 512], P('gx', 'gy', 'gz'), may hold values from 0.5 to 4
Outputs:
- correction: float32 [128, 128, 256], P('gx', 'gy', 'gz')
Inputs may be any that keep to these rules, and one draw needn't show every extreme that they name: `nnc_cell`: x * 128 + z of a cell with local x and local layer z on the device's first y layer. `nnc_remote`: x * 256 + z2, with x the same local x as nnc_cell and z2 a global layer, naming a cell on the last y layer of the device below in y. `nnc_mask`: each device's live slots come first, then zeros; every slot is 0 on devices of the first gy index; the device last along every axis has all slots live.
All inputs are finite; a program needn't handle non-finite values.
Results may differ from a plain program's by a relative error of at most 0.00002.
Values sent between devices are 32-bit elements; how exact they have to be, the bound alone decides.
A program may use at most 64 MiB of HBM per device.

v0:
```python
import functools
import jax
import jax.numpy as jnp
from jax import lax
from jax.experimental import pallas as pl
from jax.experimental.pallas import tpu as pltpu
from jax.sharding import PartitionSpec as P

SWEEPS = 6
lam_low = 0.1
lam_high = 2.0
F32 = jnp.float32
BF16 = jnp.bfloat16
UNROLL = 4
MESH = pl.DeviceIdType.MESH


def harmonic(left, right):
    return 2.0 * (left * right) / (left + right)


def parts_of(value):
    high = value.astype(BF16).astype(F32)
    rest = value - high
    middle = rest.astype(BF16).astype(F32)
    return high, middle, rest - middle


def stacked(value):
    return jnp.concatenate(parts_of(value), axis=0).astype(BF16)


def one_hot(row, count, kind):
    slots = row.shape[1]
    rows = lax.broadcasted_iota(jnp.int32, (count, slots), 0)
    return jnp.where(rows == row, 1.0, 0.0).astype(kind)


def gathered(face, columns3, layers):
    picked = lax.dot_general(
        stacked(face), columns3, (((0,), (0,)), ((), ())), preferred_element_type=F32
    )
    return jnp.sum(picked * layers, axis=0, keepdims=True)


def scattered(row, columns3, layers):
    depth_x = columns3.shape[0] // 3
    columns = columns3[0:depth_x, :].astype(F32)
    left = jnp.concatenate([columns * part for part in parts_of(row)], axis=0).astype(BF16)
    out = lax.dot_general(left, layers, (((1,), (1,)), ((), ())), preferred_element_type=F32)
    return out[0:depth_x] + out[depth_x : 2 * depth_x] + out[2 * depth_x :]


def kernel(
    sizes, rhs, acc, perm, cell_ref, remote_ref, mask_ref, trans_ref, out,
    c0, c1, inv, g, tx, ty, tz, hy, hyt, hz, hzt,
    ystage, zstage, xland, yland, zland, liststage, listland,
    own_x3, own_z, own_col, up_x3, up_z, up_own,
    xs, xr, ys, yr, zs, zr, ls, lr,
):
    nx, ny, nz = sizes
    dx, dy, dz = rhs.shape
    i, j, l = lax.axis_index("gx"), lax.axis_index("gy"), lax.axis_index("gz")
    column = dz * nz
    if nz == 2:
        z_sides = [((dz - 1) * (1 - l), 1 - l, l >= 0, 0)]
    else:
        z_sides = [(dz - 1, l + 1, l < nz - 1, 0), (0, l - 1, l > 0, 1)]
    x_sides = [(i - 1, i > 0), (i + 1, i < nx - 1)]
    y_sides = [(j - 1, j > 0), (j + 1, j < ny - 1)]

    barrier = pltpu.get_barrier_semaphore()

    def greet(ok, peer):
        @pl.when(ok)
        def _():
            pl.semaphore_signal(barrier, inc=1, device_id=peer, device_id_type=MESH)

        return jnp.where(ok, 1, 0)

    count = 0
    for peer, ok in x_sides:
        count = count + greet(ok, (peer, j, l))
    for peer, ok in y_sides:
        for other in range(nz):
            count = count + greet(ok, (i, peer, other))
    for _, peer, ok, _ in z_sides:
        count = count + greet(ok, (i, j, peer))

    lane = lax.broadcasted_iota(jnp.int32, (dy, dz), 1)
    row = lax.broadcasted_iota(jnp.int32, (dy, dz), 0)

    def pack_shift(x, edge):
        return lax.rem(x + dz - edge, dz)

    def unpack_shift(x, edge):
        return lax.rem(edge + dz - x, dz)

    def pack_into(packs, x, plane):
        return tuple(
            jnp.where(lane == x, pltpu.roll(plane, pack_shift(x, side[0]), 1), p)
            for p, side in zip(packs, z_sides)
        )

    def unpacked(values, x):
        total = 0.0
        for v, side in zip(values, z_sides):
            total = total + jnp.where(
                lane == side[0], pltpu.roll(v, unpack_shift(x, side[0]), 1), 0.0
            )
        return total

    zero_packs = tuple(jnp.zeros((dy, dz), F32) for _ in z_sides)

    def planes(body, carry):
        def step(s, carry):
            for u in range(UNROLL):
                carry = body(s * UNROLL + u, carry)
            return carry

        return lax.fori_loop(0, dx // UNROLL, step, carry)

    def copies(e, x_src):
        sends, receives = [], []
        for side in range(2):
            peer, ok = x_sides[side]
            sends.append((ok, pltpu.make_async_remote_copy(
                x_src[side], xland.at[e, 1 - side], xs.at[e, side], xr.at[e, 1 - side],
                device_id=(peer, j, l), device_id_type=MESH)))
            receives.append((ok, pltpu.make_async_remote_copy(
                x_src[side], xland.at[e, side], xs.at[e, side], xr.at[e, side],
                device_id=(peer, j, l), device_id_type=MESH)))
        for side in range(2):
            peer, ok = y_sides[side]
            for other in range(nz):
                sends.append((ok, pltpu.make_async_remote_copy(
                    ystage.at[e, side], yland.at[e, 1 - side, l],
                    ys.at[e, side, other], yr.at[e, 1 - side, l],
                    device_id=(i, peer, other), device_id_type=MESH)))
                receives.append((ok, pltpu.make_async_remote_copy(
                    ystage.at[e, side], yland.at[e, side, other],
                    ys.at[e, side, other], yr.at[e, side, other],
                    device_id=(i, peer, other), device_id_type=MESH)))
        for _, peer, ok, side in z_sides:
            far = side if len(z_sides) == 1 else 1 - side
            sends.append((ok, pltpu.make_async_remote_copy(
                zstage.at[e, side], zland.at[e, far], zs.at[e, side], zr.at[e, far],
                device_id=(i, j, peer), device_id_type=MESH)))
            receives.append((ok, pltpu.make_async_remote_copy(
                zstage.at[e, side], zland.at[e, side], zs.at[e, side], zr.at[e, side],
                device_id=(i, j, peer), device_id_type=MESH)))
        return sends, receives

    def each(pairs, act):
        for ok, copy in pairs:
            @pl.when(ok)
            def _(copy=copy):
                act(copy)

    cell, remote = cell_ref[...], remote_ref[...]
    weight = trans_ref[...] * mask_ref[...].astype(F32)
    slots = cell.shape[1]
    liststage[...] = jnp.zeros_like(liststage)
    liststage[0:1, :] = cell.astype(F32)
    liststage[1:2, :] = remote.astype(F32)
    liststage[2:3, :] = weight

    def first(x, packs):
        ystage[0, 0, pl.ds(x, 1), :] = perm[1, x, 0:1, :]
        ystage[0, 1, pl.ds(x, 1), :] = perm[1, x, dy - 1 : dy, :]
        return pack_into(packs, x, perm[2, x])

    packs = planes(first, zero_packs)
    for side, p in enumerate(packs):
        zstage[0, side] = p

    for side in range(2):
        @pl.when(jnp.logical_not(x_sides[side][1]))
        def _(side=side):
            for e in range(SWEEPS):
                xland[e, side] = jnp.zeros((dy, dz), F32)

        @pl.when(jnp.logical_not(y_sides[side][1]))
        def _(side=side):
            for e in range(SWEEPS):
                for other in range(nz):
                    yland[e, side, other] = jnp.zeros((dx, dz), F32)
            if side == 1:
                listland[...] = jnp.zeros_like(listland)
    if nz != 2:
        for _, _, ok, side in z_sides:
            @pl.when(jnp.logical_not(ok))
            def _(side=side):
                for e in range(SWEEPS):
                    zland[e, side] = jnp.zeros((dy, dz), F32)

    pl.semaphore_wait(barrier, count)
    sends, receives = copies(0, (perm.at[0, 0], perm.at[0, dx - 1]))
    for other in range(nz):
        sends.append((y_sides[0][1], pltpu.make_async_remote_copy(
            liststage, listland.at[l], ls.at[other], lr.at[l],
            device_id=(i, j - 1, other), device_id_type=MESH)))
        receives.append((y_sides[1][1], pltpu.make_async_remote_copy(
            liststage, listland.at[other], ls.at[other], lr.at[other],
            device_id=(i, j + 1, other), device_id_type=MESH)))
    each(sends, lambda copy: copy.start())
    pending = sends

    shift_z, shift_c = dz.bit_length() - 1, column.bit_length() - 1
    own_rows = one_hot(cell >> shift_z, dx, F32)
    own_x3[...] = jnp.concatenate([own_rows] * 3, axis=0).astype(BF16)
    own_z[...] = one_hot(cell & (dz - 1), dz, BF16)
    own_col[...] = one_hot(remote & (column - 1), column, F32)
    near = scattered(weight, own_x3[...], own_z[...])

    def inner(x, carry):
        @pl.when(x < dx - 1)
        def _():
            tx[x + 1] = harmonic(perm[0, x], perm[0, x + 1])

        k = perm[1, x]
        ty[x] = jnp.where(row == dy - 1, 0.0, harmonic(k, pltpu.roll(k, dy - 1, 0)))
        k = perm[2, x]
        tz[x] = jnp.where(lane == dz - 1, 0.0, harmonic(k, pltpu.roll(k, dz - 1, 1)))
        return carry

    lax.fori_loop(0, dx, inner, 0)

    each(receives, lambda copy: copy.wait_recv())
    tx[0] = harmonic(perm[0, 0], xland[0, 0])
    tx[dx] = harmonic(perm[0, dx - 1], xland[0, 1])
    up_rows = []
    far = 0.0
    for other in range(nz):
        up_cell = listland[other, 0:1, :].astype(jnp.int32)
        up_remote = listland[other, 1:2, :].astype(jnp.int32)
        up_weight = listland[other, 2:3, :]
        rows = one_hot(up_cell >> shift_z, dx, F32)
        up_x3[other] = jnp.concatenate([rows] * 3, axis=0).astype(BF16)
        up_z[other] = one_hot(up_cell & (dz - 1), dz, F32)
        up_own[other] = one_hot((up_remote & (column - 1)) - l * dz, dz, BF16)
        far = far + scattered(up_weight, up_x3[other], up_own[other])
    for side, extra in ((0, near), (1, far)):
        value = 0.0
        for other in range(nz):
            value = jnp.where(l == other, yland[0, side, other], value)
        t = harmonic(ystage[0, side], value)
        hyt[side] = t
        hy[side] = t + extra
    ztotal = []
    for side in range(len(z_sides)):
        t = harmonic(zstage[0, side], zland[0, side])
        hzt[side] = t
        ztotal.append(t)

    theta = (lam_high + lam_low) / 2.0
    delta = (lam_high - lam_low) / 2.0
    sigma = theta / delta

    def faced(x):
        return jnp.where(row == 0, hy[0, pl.ds(x, 1), :], 0.0) + jnp.where(
            row == dy - 1, hy[1, pl.ds(x, 1), :], 0.0
        )

    def stage(e, x, plane, packs):
        ystage[e, 0, pl.ds(x, 1), :] = plane[0:1, :]
        ystage[e, 1, pl.ds(x, 1), :] = plane[dy - 1 : dy, :]
        return pack_into(packs, x, plane)

    def begin(x, packs):
        y, z = ty[x], tz[x]
        diagonal = acc[x] + (tx[x] + tx[x + 1]) + (y + pltpu.roll(y, 1, 0))
        diagonal = diagonal + (z + pltpu.roll(z, 1, 1)) + faced(x) + unpacked(ztotal, x)
        inverse = 1.0 / diagonal
        value = inverse * rhs[x]
        inv[x] = inverse
        g[x] = value
        value = value / theta
        c0[x + 1] = value
        return stage(1, x, value, packs)

    packs = planes(begin, zero_packs)
    now, before = c0, c1
    rho = 1.0 / sigma
    for e in range(1, SWEEPS):
        each(pending, lambda copy: copy.wait_send())
        for side, p in enumerate(packs):
            zstage[e, side] = p
        sends, receives = copies(e, (now.at[1], now.at[dx]))
        each(sends, lambda copy: copy.start())
        pending = sends
        each(receives, lambda copy: copy.wait_recv())
        now[0] = xland[e, 0]
        now[dx + 1] = xland[e, 1]
        flux = 0.0
        far = 0.0
        sides = [0.0, 0.0]
        for other in range(nz):
            rows = slice(other * dz, (other + 1) * dz)
            flux = flux + gathered(yland[e, 0, other], own_x3[...], own_col[rows, :])
            up = listland[other, 2:3, :] * gathered(yland[e, 1, other], up_x3[other], up_z[other])
            far = far + scattered(up, up_x3[other], up_own[other])
            for side in range(2):
                sides[side] = jnp.where(l == other, yland[e, side, other], sides[side])
        near = scattered(weight * flux, own_x3[...], own_z[...])
        hy[0] = hyt[0] * sides[0] + near
        hy[1] = hyt[1] * sides[1] + far
        zvalues = [hzt[side] * zland[e, side] for side in range(len(z_sides))]

        rho_next = 1.0 / (2.0 * sigma - rho)
        a, b = rho_next * rho, 2.0 * rho_next / delta
        rho = rho_next

        def sweep(x, packs, e=e, now=now, before=before, a=a, b=b, zvalues=zvalues):
            v = now[x + 1]
            y, z = ty[x], tz[x]
            total = tx[x + 1] * now[x + 2] + tx[x] * now[x]
            total = total + (y * pltpu.roll(v, dy - 1, 0) + pltpu.roll(y * v, 1, 0))
            total = total + (z * pltpu.roll(v, dz - 1, 1) + pltpu.roll(z * v, 1, 1))
            total = total + faced(x) + unpacked(zvalues, x)
            new = (1.0 + a - b) * v + b * (g[x] + inv[x] * total)
            if e > 1:
                new = new - a * before[x + 1]
            if e == SWEEPS - 1:
                out[x] = new
                return packs
            before[x + 1] = new
            return stage(e + 1, x, new, packs)

        packs = planes(sweep, zero_packs)
        now, before = before, now
    each(pending, lambda copy: copy.wait_send())


def local(sizes, rhs, accumulation, permeability, nnc_cell, nnc_remote, nnc_mask, nnc_trans):
    nx, ny, nz = sizes
    dx, dy, dz = rhs.shape
    slots = nnc_cell.shape[-1]
    column = dz * nz
    plane = (dx, dy, dz)
    zn = 1 if nz == 2 else 2
    vmem = pl.BlockSpec(memory_space=pltpu.VMEM)
    dma = pltpu.SemaphoreType.DMA
    V = pltpu.VMEM
    scratch = [
        V((dx + 2, dy, dz), F32), V((dx + 2, dy, dz), F32),
        V(plane, F32), V(plane, F32),
        V((dx + 1, dy, dz), F32), V(plane, F32), V(plane, F32),
        V((2, dx, dz), F32), V((2, dx, dz), F32),
        V((zn, dy, dz), F32), V((zn, dy, dz), F32),
        V((SWEEPS, 2, dx, dz), F32), V((SWEEPS, zn, dy, dz), F32),
        V((SWEEPS, 2, dy, dz), F32), V((SWEEPS, 2, nz, dx, dz), F32),
        V((SWEEPS, zn, dy, dz), F32),
        V((8, slots), F32), V((nz, 8, slots), F32),
        V((3 * dx, slots), BF16), V((dz, slots), BF16), V((column, slots), F32),
        V((nz, 3 * dx, slots), BF16), V((nz, dz, slots), F32), V((nz, dz, slots), BF16),
        dma((SWEEPS, 2)), dma((SWEEPS, 2)),
        dma((SWEEPS, 2, nz)), dma((SWEEPS, 2, nz)),
        dma((SWEEPS, zn)), dma((SWEEPS, zn)),
        dma((nz,)), dma((nz,)),
    ]
    return pl.pallas_call(
        functools.partial(kernel, sizes),
        out_shape=jax.ShapeDtypeStruct(plane, F32),
        in_specs=[vmem] * 7,
        out_specs=vmem,
        scratch_shapes=scratch,
        compiler_params=pltpu.CompilerParams(
            collective_id=0, has_side_effects=True, vmem_limit_bytes=48 * 1024 * 1024
        ),
    )(
        rhs, accumulation, permeability,
        *(v.reshape(1, slots) for v in (nnc_cell, nnc_remote, nnc_mask, nnc_trans)),
    )


def solution(mesh):
    sizes = tuple(mesh.shape[name] for name in ("gx", "gy", "gz"))
    cells = P("gx", "gy", "gz")
    lists = P("gx", "gy", "gz", None)
    return jax.shard_map(
        functools.partial(local, sizes),
        mesh=mesh,
        in_specs=(cells, cells, P(None, "gx", "gy", "gz"), lists, lists, lists, lists),
        out_specs=cells,
        check_vma=False,
    )
```

profile of v0, /device:TPU:0, one launch (start us, length us, event | category | flops | bytes accessed | tf_op | source)
XLA Modules:
  0.0 43.2 jit_solution(5923005066508575657)
XLA Ops:
  0.0 0.0 copy-start
  0.0 1.4 %copy-done = f32[3,32,32,128]{3,2,1,0:T(8,128)S(1)} copy-done((f32[3,32,32,128]{3,2,1,0:T(8,128)S(1)}, f32[3,32,32,128]{3,2,1,0:T(8,128)}, u32[]{:S(2)}) %copy-start) | copy-done | bytes 1572888
  1.4 0.0 copy-start.1
  1.4 1.0 %copy-done.1 = f32[32,32,128]{2,1,0:T(8,128)S(1)} copy-done((f32[32,32,128]{2,1,0:T(8,128)S(1)}, f32[32,32,128]{2,1,0:T(8,128)}, u32[]{:S(2)}) %copy-start.1) | copy-done | bytes 524312
  2.5 0.0 copy-start.2
  2.5 1.0 %copy-done.2 = f32[32,32,128]{2,1,0:T(8,128)S(1)} copy-done((f32[32,32,128]{2,1,0:T(8,128)S(1)}, f32[32,32,128]{2,1,0:T(8,128)}, u32[]{:S(2)}) %copy-start.2) | copy-done | bytes 524312
  3.5 0.0 copy-start.3
  3.5 0.7 %copy-done.3 = s32[1,1,1,512]{3,2,1,0:T(1,128)S(1)} copy-done((s32[1,1,1,512]{3,2,1,0:T(1,128)S(1)}, s32[1,1,1,512]{3,2,1,0:T(1,128)}, u32[]{:S(2)}) %copy-start.3) | copy-done | bytes 2072
  4.2 0.0 copy-start.4
  4.2 0.7 %copy-done.4 = s32[1,1,1,512]{3,2,1,0:T(1,128)S(1)} copy-done((s32[1,1,1,512]{3,2,1,0:T(1,128)S(1)}, s32[1,1,1,512]{3,2,1,0:T(1,128)}, u32[]{:S(2)}) %copy-start.4) | copy-done | bytes 2072
  4.9 0.0 copy-start.5
  4.9 0.7 %copy-done.5 = s32[1,1,1,512]{3,2,1,0:T(1,128)S(1)} copy-done((s32[1,1,1,512]{3,2,1,0:T(1,128)S(1)}, s32[1,1,1,512]{3,2,1,0:T(1,128)}, u32[]{:S(2)}) %copy-start.5) | copy-done | bytes 2072
  5.5 0.0 copy-start.6
  5.5 0.7 %copy-done.6 = f32[1,1,1,512]{3,2,1,0:T(1,128)S(1)} copy-done((f32[1,1,1,512]{3,2,1,0:T(1,128)S(1)}, f32[1,1,1,512]{3,2,1,0:T(1,128)}, u32[]{:S(2)}) %copy-start.6) | copy-done | bytes 2072
  6.2 36.2 %shard_map.73 = f32[32,32,128]{2,1,0:T(8,128)S(1)} custom-call(f32[32,32,128]{2,1,0:T(8,128)S(1)} %copy-done.1, f32[32,32,128]{2,1,0:T(8,128)S(1)} %copy-done.2, f32[3,32,32,128]{3,2,1,0:T(8,128)S(1)} %copy-done, s32[1,512]{1,0:T(1,128)S(1)} %bitcast.4, s32[1,512]{1,0:T(1,128)S(1)} %bitcast.5, s32[1,512]{1,0:T(1,128)S(1)} %bitcast.6, f32[1,512]{1,0:T(1,128)S(1)} %bitcast.7), custom_call_target="tpu_custom_call" | custom-call | tf_op jit(solution)/shard_map/pallas_call | solution.py:362
  42.5 0.8 %copy.9 = f32[32,32,128]{2,1,0:T(8,128)} copy(f32[32,32,128]{2,1,0:T(8,128)S(1)} %shard_map.73) | data formatting | bytes 1048576
Async XLA Ops:
  0.0 1.4 %copy-start = (f32[3,32,32,128]{3,2,1,0:T(8,128)S(1)}, f32[3,32,32,128]{3,2,1,0:T(8,128)}, u32[]{:S(2)}) copy-start(f32[3,32,32,128]{3,2,1,0:T(8,128)} %perm.1) | copy-start | bytes 4718596
  1.4 1.0 %copy-start.1 = (f32[32,32,128]{2,1,0:T(8,128)S(1)}, f32[32,32,128]{2,1,0:T(8,128)}, u32[]{:S(2)}) copy-start(f32[32,32,128]{2,1,0:T(8,128)} %rhs.1) | copy-start | bytes 1572868
  2.5 1.0 %copy-start.2 = (f32[32,32,128]{2,1,0:T(8,128)S(1)}, f32[32,32,128]{2,1,0:T(8,128)}, u32[]{:S(2)}) copy-start(f32[32,32,128]{2,1,0:T(8,128)} %acc.1) | copy-start | bytes 1572868
  3.5 0.7 %copy-start.3 = (s32[1,1,1,512]{3,2,1,0:T(1,128)S(1)}, s32[1,1,1,512]{3,2,1,0:T(1,128)}, u32[]{:S(2)}) copy-start(s32[1,1,1,512]{3,2,1,0:T(1,128)} %param.10) | copy-start | bytes 6148
  4.2 0.7 %copy-start.4 = (s32[1,1,1,512]{3,2,1,0:T(1,128)S(1)}, s32[1,1,1,512]{3,2,1,0:T(1,128)}, u32[]{:S(2)}) copy-start(s32[1,1,1,512]{3,2,1,0:T(1,128)} %param.11) | copy-start | bytes 6148
  4.9 0.7 %copy-start.5 = (s32[1,1,1,512]{3,2,1,0:T(1,128)S(1)}, s32[1,1,1,512]{3,2,1,0:T(1,128)}, u32[]{:S(2)}) copy-start(s32[1,1,1,512]{3,2,1,0:T(1,128)} %param.12) | copy-start | bytes 6148
  5.5 0.7 %copy-start.6 = (f32[1,1,1,512]{3,2,1,0:T(1,128)S(1)}, f32[1,1,1,512]{3,2,1,0:T(1,128)}, u32[]{:S(2)}) copy-start(f32[1,1,1,512]{3,2,1,0:T(1,128)} %param.13) | copy-start | bytes 6148
where the time goes:
time: 43.6 us; the launch traced here: 43.2 us
  Pallas kernels  36.2 us (83%)
  local copies, waits for them, and re-layouts  7.01 us (16%)
    pallas_call x1, Pallas kernels, local(): pl.pallas_call(functools.partial(kernel, sizes), out_shape=jax.ShapeDtype...  36.2 us
    unnamed x15, local copies, waits for them, and re-layouts  7.01 us

commit v1 on v0

--- a/solution.py
+++ b/solution.py
@@ -52,9 +52,10 @@
 
 
 def kernel(
-    sizes, rhs, acc, perm, cell_ref, remote_ref, mask_ref, trans_ref, out,
-    c0, c1, inv, g, tx, ty, tz, hy, hyt, hz, hzt,
-    ystage, zstage, xland, yland, zland, liststage, listland,
+    sizes, rhs_in, acc_in, perm_in, cell_in, remote_in, mask_in, trans_in, out,
+    rhs, acc, perm, cell_ref, remote_ref, mask_ref, trans_ref, load,
+    c0, c1, inv, g, tx, ty, tz, hx, hxt, hy, hyt, hz, hzt, yinv, zinv, ypart, turn,
+    xstage, ystage, zstage, xland, yland, zland, liststage, listland,
     own_x3, own_z, own_col, up_x3, up_z, up_own,
     xs, xr, ys, yr, zs, zr, ls, lr,
 ):
@@ -68,6 +69,15 @@
         z_sides = [(dz - 1, l + 1, l < nz - 1, 0), (0, l - 1, l > 0, 1)]
     x_sides = [(i - 1, i > 0), (i + 1, i < nx - 1)]
     y_sides = [(j - 1, j > 0), (j + 1, j < ny - 1)]
+
+    loads = [
+        pltpu.make_async_copy(src, dst, load.at[index])
+        for index, (src, dst) in enumerate((
+            (cell_in, cell_ref), (remote_in, remote_ref), (mask_in, mask_ref),
+            (trans_in, trans_ref), (perm_in, perm), (acc_in, acc), (rhs_in, rhs)))
+    ]
+    for copy in loads:
+        copy.start()
 
     barrier = pltpu.get_barrier_semaphore()
 
@@ -157,6 +167,8 @@
             def _(copy=copy):
                 act(copy)
 
+    for copy in loads[:4]:
+        copy.wait()
     cell, remote = cell_ref[...], remote_ref[...]
     weight = trans_ref[...] * mask_ref[...].astype(F32)
     slots = cell.shape[1]
@@ -164,6 +176,11 @@
     liststage[0:1, :] = cell.astype(F32)
     liststage[1:2, :] = remote.astype(F32)
     liststage[2:3, :] = weight
+
+    for ref in (c0, c1):
+        ref[0] = jnp.zeros((dy, dz), F32)
+        ref[dx + 1] = jnp.zeros((dy, dz), F32)
+    loads[4].wait()
 
     def first(x, packs):
         ystage[0, 0, pl.ds(x, 1), :] = perm[1, x, 0:1, :]
@@ -227,6 +244,8 @@
     lax.fori_loop(0, dx, inner, 0)
 
     each(receives, lambda copy: copy.wait_recv())
+    for copy in loads[5:]:
+        copy.wait()
     tx[0] = harmonic(perm[0, 0], xland[0, 0])
     tx[dx] = harmonic(perm[0, dx - 1], xland[0, 1])
     up_rows = []
@@ -249,7 +268,7 @@
         hy[side] = t + extra
     ztotal = []
     for side in range(len(z_sides)):
-        t = harmonic(zstage[0, side], zland[0, side])
+        t = jnp.where(lane < dx, harmonic(zstage[0, side], zland[0, side]), 0.0)
         hzt[side] = t
         ztotal.append(t)
 
@@ -262,36 +281,83 @@
             row == dy - 1, hy[1, pl.ds(x, 1), :], 0.0
         )
 
-    def stage(e, x, plane, packs):
-        ystage[e, 0, pl.ds(x, 1), :] = plane[0:1, :]
-        ystage[e, 1, pl.ds(x, 1), :] = plane[dy - 1 : dy, :]
-        return pack_into(packs, x, plane)
-
-    def begin(x, packs):
+    def rims(x, values):
+        return faced(x) + unpacked(values, x)
+
+    def put_rows(ref, x, plane):
+        ref[0, pl.ds(x, 1), :] = plane[0:1, :]
+        ref[1, pl.ds(x, 1), :] = plane[dy - 1 : dy, :]
+
+    def begin(x, carry):
+        packs, inv_packs = carry
         y, z = ty[x], tz[x]
         diagonal = acc[x] + (tx[x] + tx[x + 1]) + (y + pltpu.roll(y, 1, 0))
-        diagonal = diagonal + (z + pltpu.roll(z, 1, 1)) + faced(x) + unpacked(ztotal, x)
+        diagonal = diagonal + (z + pltpu.roll(z, 1, 1)) + rims(x, ztotal)
         inverse = 1.0 / diagonal
         value = inverse * rhs[x]
         inv[x] = inverse
         g[x] = value
         value = value / theta
         c0[x + 1] = value
-        return stage(1, x, value, packs)
-
-    packs = planes(begin, zero_packs)
+        put_rows(ystage.at[1], x, value)
+        put_rows(yinv, x, inverse)
+        return pack_into(packs, x, value), pack_into(inv_packs, x, inverse)
+
+    packs, inv_packs = planes(begin, (zero_packs, zero_packs))
+    for side in range(len(z_sides)):
+        zstage[1, side] = packs[side]
+        zinv[side] = inv_packs[side]
+    xstage[1, 0] = c0[1]
+    xstage[1, 1] = c0[dx]
+    for side, edge in ((0, 0), (1, dx)):
+        hxt[side] = tx[edge]
+        tx[edge] = jnp.zeros((dy, dz), F32)
+
+    square = dz - 2 * dx
     now, before = c0, c1
     rho = 1.0 / sigma
+    b = 0.0
     for e in range(1, SWEEPS):
         each(pending, lambda copy: copy.wait_send())
-        for side, p in enumerate(packs):
-            zstage[e, side] = p
-        sends, receives = copies(e, (now.at[1], now.at[dx]))
+        sends, receives = copies(e, (xstage.at[e, 0], xstage.at[e, 1]))
         each(sends, lambda copy: copy.start())
         pending = sends
+
+        rho_next = 1.0 / (2.0 * sigma - rho)
+        a, b_old, b = rho_next * rho, b, 2.0 * rho_next / delta
+        rho = rho_next
+        if e > 1:
+            now[1] = xstage[e, 0]
+            now[dx] = xstage[e, 1]
+
+        def bulk(x, packs, fix, e=e, now=now, before=before, a=a, b=b, b_old=b_old):
+            if fix and e > 1:
+                values = [hz[side] for side in range(len(z_sides))]
+                now[x + 2] = now[x + 2] + b_old * inv[x + 1] * rims(x + 1, values)
+            v = now[x + 1]
+            y, z = ty[x], tz[x]
+            total = tx[x + 1] * now[x + 2] + tx[x] * now[x]
+            total = total + (y * pltpu.roll(v, dy - 1, 0) + pltpu.roll(y * v, 1, 0))
+            total = total + (z * pltpu.roll(v, dz - 1, 1) + pltpu.roll(z * v, 1, 1))
+            new = (1.0 + a - b) * v + b * (g[x] + inv[x] * total)
+            if e > 1:
+                new = new - a * before[x + 1]
+            before[x + 1] = new
+            if e == SWEEPS - 1:
+                return packs
+            put_rows(ypart, x, new)
+            return pack_into(packs, x, new)
+
+        def group(step, packs, bulk=bulk):
+            for u in range(UNROLL):
+                packs = bulk(step * UNROLL + u, packs, True)
+            return packs
+
+        packs = lax.fori_loop(0, dx // UNROLL - 1, group, zero_packs)
+        for x in range(dx - UNROLL, dx):
+            packs = bulk(x, packs, x < dx - 2)
+
         each(receives, lambda copy: copy.wait_recv())
-        now[0] = xland[e, 0]
-        now[dx + 1] = xland[e, 1]
         flux = 0.0
         far = 0.0
         sides = [0.0, 0.0]
@@ -303,31 +369,56 @@
             for side in range(2):
                 sides[side] = jnp.where(l == other, yland[e, side, other], sides[side])
         near = scattered(weight * flux, own_x3[...], own_z[...])
-        hy[0] = hyt[0] * sides[0] + near
-        hy[1] = hyt[1] * sides[1] + far
+        yvalues = [hyt[0] * sides[0] + near, hyt[1] * sides[1] + far]
+        for side in range(2):
+            hy[side] = yvalues[side]
+            hx[side] = hxt[side] * xland[e, side]
         zvalues = [hzt[side] * zland[e, side] for side in range(len(z_sides))]
-
-        rho_next = 1.0 / (2.0 * sigma - rho)
-        a, b = rho_next * rho, 2.0 * rho_next / delta
-        rho = rho_next
-
-        def sweep(x, packs, e=e, now=now, before=before, a=a, b=b, zvalues=zvalues):
-            v = now[x + 1]
-            y, z = ty[x], tz[x]
-            total = tx[x + 1] * now[x + 2] + tx[x] * now[x]
-            total = total + (y * pltpu.roll(v, dy - 1, 0) + pltpu.roll(y * v, 1, 0))
-            total = total + (z * pltpu.roll(v, dz - 1, 1) + pltpu.roll(z * v, 1, 1))
-            total = total + faced(x) + unpacked(zvalues, x)
-            new = (1.0 + a - b) * v + b * (g[x] + inv[x] * total)
-            if e > 1:
-                new = new - a * before[x + 1]
-            if e == SWEEPS - 1:
-                out[x] = new
-                return packs
-            before[x + 1] = new
-            return stage(e + 1, x, new, packs)
-
-        packs = planes(sweep, zero_packs)
+        for side in range(len(z_sides)):
+            hz[side] = zvalues[side]
+
+        ends = []
+        for side, x in ((0, 0), (1, dx - 1)):
+            ends.append(before[x + 1] + b * inv[x] * (hx[side] + rims(x, zvalues)))
+        if e == SWEEPS - 1:
+            out[0] = ends[0]
+            out[dx - 1] = ends[1]
+
+            def last(x, carry, before=before, b=b):
+                values = [hz[side] for side in range(len(z_sides))]
+                out[x] = before[x + 1] + b * inv[x] * rims(x, values)
+                return carry
+
+            lax.fori_loop(1, dx - 1, last, 0)
+            continue
+        xstage[e + 1, 0] = ends[0]
+        xstage[e + 1, 1] = ends[1]
+        xrow = lax.broadcasted_iota(jnp.int32, (dx, dz), 0)
+        xlane = lax.broadcasted_iota(jnp.int32, (dx, dz), 1)
+        turned = [
+            jnp.concatenate([v, jnp.zeros((dz - dy, dz), F32)], axis=0).T[0:dx, :]
+            for v in zvalues
+        ]
+        for side, y in ((0, 0), (1, dy - 1)):
+            term = yvalues[side]
+            term = term + jnp.where(xrow == 0, hx[0, y : y + 1, :], 0.0)
+            term = term + jnp.where(xrow == dx - 1, hx[1, y : y + 1, :], 0.0)
+            for t, (edge, _, _, _) in zip(turned, z_sides):
+                shifted = pltpu.roll(t, lax.rem(edge + dz - y, dz), 1)
+                term = term + jnp.where(xlane == edge, shifted, 0.0)
+            ystage[e + 1, side] = ypart[side] + b * yinv[side] * term
+        turn[...] = jnp.concatenate(yvalues + [jnp.zeros((square, dz), F32)], axis=0).T
+        for (edge, _, _, zside), p in zip(z_sides, packs):
+            line = turn[pl.ds(edge, 1), :]
+            line = jnp.broadcast_to(line, (8, dz))
+            upper = pltpu.roll(line, dz - dx, 1)
+            term = zvalues[zside]
+            term = term + jnp.where(row == 0, line[0:1, :], 0.0)
+            term = term + jnp.where(row == dy - 1, upper[0:1, :], 0.0)
+            for side, x in ((0, 0), (1, dx - 1)):
+                shifted = pltpu.roll(hx[side], pack_shift(x, edge), 1)
+                term = term + jnp.where(lane == x, shifted, 0.0)
+            zstage[e + 1, zside] = p + b * zinv[zside] * term
         now, before = before, now
     each(pending, lambda copy: copy.wait_send())
 
@@ -340,14 +431,20 @@
     plane = (dx, dy, dz)
     zn = 1 if nz == 2 else 2
     vmem = pl.BlockSpec(memory_space=pltpu.VMEM)
+    hbm = pl.BlockSpec(memory_space=pltpu.HBM)
     dma = pltpu.SemaphoreType.DMA
     V = pltpu.VMEM
     scratch = [
+        V(plane, F32), V(plane, F32), V((3, *plane), F32),
+        V((1, slots), jnp.int32), V((1, slots), jnp.int32), V((1, slots), jnp.int32),
+        V((1, slots), F32), dma((7,)),
         V((dx + 2, dy, dz), F32), V((dx + 2, dy, dz), F32),
         V(plane, F32), V(plane, F32),
         V((dx + 1, dy, dz), F32), V(plane, F32), V(plane, F32),
-        V((2, dx, dz), F32), V((2, dx, dz), F32),
+        V((2, dy, dz), F32), V((2, dy, dz), F32), V((2, dx, dz), F32), V((2, dx, dz), F32),
         V((zn, dy, dz), F32), V((zn, dy, dz), F32),
+        V((2, dx, dz), F32), V((zn, dy, dz), F32), V((2, dx, dz), F32), V((dz, dz), F32),
+        V((SWEEPS, 2, dy, dz), F32),
         V((SWEEPS, 2, dx, dz), F32), V((SWEEPS, zn, dy, dz), F32),
         V((SWEEPS, 2, dy, dz), F32), V((SWEEPS, 2, nz, dx, dz), F32),
         V((SWEEPS, zn, dy, dz), F32),
@@ -362,7 +459,7 @@
     return pl.pallas_call(
         functools.partial(kernel, sizes),
         out_shape=jax.ShapeDtypeStruct(plane, F32),
-        in_specs=[vmem] * 7,
+        in_specs=[hbm] * 7,
         out_specs=vmem,
         scratch_shapes=scratch,
         compiler_params=pltpu.CompilerParams(

time: 43.6 us -> 39.7 us (0.911)
  Pallas kernels: 36.2 us -> 32.4 us
    pallas_call x1, Pallas kernels: 36.2 us -> 32.4 us  [local(): pl.pallas_call(functools.partial(kernel, sizes), out_shape=jax.ShapeDtype...]
where the time goes in v1:
time: 39.7 us; the launch traced here: 39.4 us
  Pallas kernels  32.4 us (82%)
  local copies, waits for them, and re-layouts  7.01 us (18%)
    pallas_call x1, Pallas kernels, local(): pl.pallas_call(functools.partial(kernel, sizes), out_shape=jax.ShapeDtype...  32.4 us
    unnamed x15, local copies, waits for them, and re-layouts  7.01 us

profile of v1, /device:TPU:0, one launch (start us, length us, event | category | flops | bytes accessed | tf_op | source)
XLA Modules:
  0.0 39.4 jit_solution(12593198304072123526)
XLA Ops:
  0.0 0.0 copy-start
  0.0 1.4 %copy-done = f32[3,32,32,128]{3,2,1,0:T(8,128)S(1)} copy-done((f32[3,32,32,128]{3,2,1,0:T(8,128)S(1)}, f32[3,32,32,128]{3,2,1,0:T(8,128)}, u32[]{:S(2)}) %copy-start) | copy-done | bytes 1572888
  1.4 0.0 copy-start.1
  1.4 1.0 %copy-done.1 = f32[32,32,128]{2,1,0:T(8,128)S(1)} copy-done((f32[32,32,128]{2,1,0:T(8,128)S(1)}, f32[32,32,128]{2,1,0:T(8,128)}, u32[]{:S(2)}) %copy-start.1) | copy-done | bytes 524312
  2.5 0.0 copy-start.2
  2.5 1.0 %copy-done.2 = f32[32,32,128]{2,1,0:T(8,128)S(1)} copy-done((f32[32,32,128]{2,1,0:T(8,128)S(1)}, f32[32,32,128]{2,1,0:T(8,128)}, u32[]{:S(2)}) %copy-start.2) | copy-done | bytes 524312
  3.5 0.0 copy-start.3
  3.5 0.7 %copy-done.3 = s32[1,1,1,512]{3,2,1,0:T(1,128)S(1)} copy-done((s32[1,1,1,512]{3,2,1,0:T(1,128)S(1)}, s32[1,1,1,512]{3,2,1,0:T(1,128)}, u32[]{:S(2)}) %copy-start.3) | copy-done | bytes 2072
  4.2 0.0 copy-start.4
  4.2 0.7 %copy-done.4 = s32[1,1,1,512]{3,2,1,0:T(1,128)S(1)} copy-done((s32[1,1,1,512]{3,2,1,0:T(1,128)S(1)}, s32[1,1,1,512]{3,2,1,0:T(1,128)}, u32[]{:S(2)}) %copy-start.4) | copy-done | bytes 2072
  4.9 0.0 copy-start.5
  4.9 0.7 %copy-done.5 = s32[1,1,1,512]{3,2,1,0:T(1,128)S(1)} copy-done((s32[1,1,1,512]{3,2,1,0:T(1,128)S(1)}, s32[1,1,1,512]{3,2,1,0:T(1,128)}, u32[]{:S(2)}) %copy-start.5) | copy-done | bytes 2072
  5.5 0.0 copy-start.6
  5.5 0.7 %copy-done.6 = f32[1,1,1,512]{3,2,1,0:T(1,128)S(1)} copy-done((f32[1,1,1,512]{3,2,1,0:T(1,128)S(1)}, f32[1,1,1,512]{3,2,1,0:T(1,128)}, u32[]{:S(2)}) %copy-start.6) | copy-done | bytes 2072
  6.2 32.4 %shard_map.73 = f32[32,32,128]{2,1,0:T(8,128)S(1)} custom-call(f32[32,32,128]{2,1,0:T(8,128)S(1)} %copy-done.1, f32[32,32,128]{2,1,0:T(8,128)S(1)} %copy-done.2, f32[3,32,32,128]{3,2,1,0:T(8,128)S(1)} %copy-done, s32[1,512]{1,0:T(1,128)S(1)} %bitcast.4, s32[1,512]{1,0:T(1,128)S(1)} %bitcast.5, s32[1,512]{1,0:T(1,128)S(1)} %bitcast.6, f32[1,512]{1,0:T(1,128)S(1)} %bitcast.7), custom_call_target="tpu_custom_call" | custom-call | tf_op jit(solution)/shard_map/pallas_call | solution.py:459
  38.6 0.8 %copy.9 = f32[32,32,128]{2,1,0:T(8,128)} copy(f32[32,32,128]{2,1,0:T(8,128)S(1)} %shard_map.73) | data formatting | bytes 1048576
Async XLA Ops:
  0.0 1.4 %copy-start = (f32[3,32,32,128]{3,2,1,0:T(8,128)S(1)}, f32[3,32,32,128]{3,2,1,0:T(8,128)}, u32[]{:S(2)}) copy-start(f32[3,32,32,128]{3,2,1,0:T(8,128)} %perm_in.1) | copy-start | bytes 4718596
  1.4 1.0 %copy-start.1 = (f32[32,32,128]{2,1,0:T(8,128)S(1)}, f32[32,32,128]{2,1,0:T(8,128)}, u32[]{:S(2)}) copy-start(f32[32,32,128]{2,1,0:T(8,128)} %rhs_in.1) | copy-start | bytes 1572868
  2.5 1.0 %copy-start.2 = (f32[32,32,128]{2,1,0:T(8,128)S(1)}, f32[32,32,128]{2,1,0:T(8,128)}, u32[]{:S(2)}) copy-start(f32[32,32,128]{2,1,0:T(8,128)} %acc_in.1) | copy-start | bytes 1572868
  3.5 0.7 %copy-start.3 = (s32[1,1,1,512]{3,2,1,0:T(1,128)S(1)}, s32[1,1,1,512]{3,2,1,0:T(1,128)}, u32[]{:S(2)}) copy-start(s32[1,1,1,512]{3,2,1,0:T(1,128)} %param.10) | copy-start | bytes 6148
  4.2 0.7 %copy-start.4 = (s32[1,1,1,512]{3,2,1,0:T(1,128)S(1)}, s32[1,1,1,512]{3,2,1,0:T(1,128)}, u32[]{:S(2)}) copy-start(s32[1,1,1,512]{3,2,1,0:T(1,128)} %param.11) | copy-start | bytes 6148
  4.9 0.7 %copy-start.5 = (s32[1,1,1,512]{3,2,1,0:T(1,128)S(1)}, s32[1,1,1,512]{3,2,1,0:T(1,128)}, u32[]{:S(2)}) copy-start(s32[1,1,1,512]{3,2,1,0:T(1,128)} %param.12) | copy-start | bytes 6148
  5.5 0.7 %copy-start.6 = (f32[1,1,1,512]{3,2,1,0:T(1,128)S(1)}, f32[1,1,1,512]{3,2,1,0:T(1,128)}, u32[]{:S(2)}) copy-start(f32[1,1,1,512]{3,2,1,0:T(1,128)} %param.13) | copy-start | bytes 6148

commit v2 on v1

--- a/solution.py
+++ b/solution.py
@@ -74,11 +74,9 @@
         pltpu.make_async_copy(src, dst, load.at[index])
         for index, (src, dst) in enumerate((
             (cell_in, cell_ref), (remote_in, remote_ref), (mask_in, mask_ref),
-            (trans_in, trans_ref), (perm_in, perm), (acc_in, acc), (rhs_in, rhs)))
+            (trans_in, trans_ref), (perm_in.at[1], perm.at[1]), (perm_in.at[2], perm.at[2]),
+            (perm_in.at[0], perm.at[0]), (acc_in, acc), (rhs_in, rhs)))
     ]
-    for copy in loads:
-        copy.start()
-
     barrier = pltpu.get_barrier_semaphore()
 
     def greet(ok, peer):
@@ -97,6 +95,9 @@
     for _, peer, ok, _ in z_sides:
         count = count + greet(ok, (i, j, peer))
 
+    for copy in loads:
+        copy.start()
+
     lane = lax.broadcasted_iota(jnp.int32, (dy, dz), 1)
     row = lax.broadcasted_iota(jnp.int32, (dy, dz), 0)
 
@@ -131,32 +132,32 @@
         return lax.fori_loop(0, dx // UNROLL, step, carry)
 
     def copies(e, x_src):
-        sends, receives = [], []
+        sends, receives = ([], [], []), ([], [], [])
         for side in range(2):
             peer, ok = x_sides[side]
-            sends.append((ok, pltpu.make_async_remote_copy(
+            sends[0].append((ok, pltpu.make_async_remote_copy(
                 x_src[side], xland.at[e, 1 - side], xs.at[e, side], xr.at[e, 1 - side],
                 device_id=(peer, j, l), device_id_type=MESH)))
-            receives.append((ok, pltpu.make_async_remote_copy(
+            receives[0].append((ok, pltpu.make_async_remote_copy(
                 x_src[side], xland.at[e, side], xs.at[e, side], xr.at[e, side],
                 device_id=(peer, j, l), device_id_type=MESH)))
         for side in range(2):
             peer, ok = y_sides[side]
             for other in range(nz):
-                sends.append((ok, pltpu.make_async_remote_copy(
+                sends[1].append((ok, pltpu.make_async_remote_copy(
                     ystage.at[e, side], yland.at[e, 1 - side, l],
                     ys.at[e, side, other], yr.at[e, 1 - side, l],
                     device_id=(i, peer, other), device_id_type=MESH)))
-                receives.append((ok, pltpu.make_async_remote_copy(
+                receives[1].append((ok, pltpu.make_async_remote_copy(
                     ystage.at[e, side], yland.at[e, side, other],
                     ys.at[e, side, other], yr.at[e, side, other],
                     device_id=(i, peer, other), device_id_type=MESH)))
         for _, peer, ok, side in z_sides:
             far = side if len(z_sides) == 1 else 1 - side
-            sends.append((ok, pltpu.make_async_remote_copy(
+            sends[2].append((ok, pltpu.make_async_remote_copy(
                 zstage.at[e, side], zland.at[e, far], zs.at[e, side], zr.at[e, far],
                 device_id=(i, j, peer), device_id_type=MESH)))
-            receives.append((ok, pltpu.make_async_remote_copy(
+            receives[2].append((ok, pltpu.make_async_remote_copy(
                 zstage.at[e, side], zland.at[e, side], zs.at[e, side], zr.at[e, side],
                 device_id=(i, j, peer), device_id_type=MESH)))
         return sends, receives
@@ -180,16 +181,6 @@
     for ref in (c0, c1):
         ref[0] = jnp.zeros((dy, dz), F32)
         ref[dx + 1] = jnp.zeros((dy, dz), F32)
-    loads[4].wait()
-
-    def first(x, packs):
-        ystage[0, 0, pl.ds(x, 1), :] = perm[1, x, 0:1, :]
-        ystage[0, 1, pl.ds(x, 1), :] = perm[1, x, dy - 1 : dy, :]
-        return pack_into(packs, x, perm[2, x])
-
-    packs = planes(first, zero_packs)
-    for side, p in enumerate(packs):
-        zstage[0, side] = p
 
     for side in range(2):
         @pl.when(jnp.logical_not(x_sides[side][1]))
@@ -212,16 +203,37 @@
                     zland[e, side] = jnp.zeros((dy, dz), F32)
 
     pl.semaphore_wait(barrier, count)
-    sends, receives = copies(0, (perm.at[0, 0], perm.at[0, dx - 1]))
+
+    def start(copy):
+        copy.start()
+
+    pending = []
+    list_sends, list_receives = [], []
     for other in range(nz):
-        sends.append((y_sides[0][1], pltpu.make_async_remote_copy(
+        list_sends.append((y_sides[0][1], pltpu.make_async_remote_copy(
             liststage, listland.at[l], ls.at[other], lr.at[l],
             device_id=(i, j - 1, other), device_id_type=MESH)))
-        receives.append((y_sides[1][1], pltpu.make_async_remote_copy(
+        list_receives.append((y_sides[1][1], pltpu.make_async_remote_copy(
             liststage, listland.at[other], ls.at[other], lr.at[other],
             device_id=(i, j + 1, other), device_id_type=MESH)))
-    each(sends, lambda copy: copy.start())
-    pending = sends
+    each(list_sends, start)
+    pending += list_sends
+    sends, receives = copies(0, (perm_in.at[0, 0], perm_in.at[0, dx - 1]))
+    each(sends[0], start)
+
+    for copy in loads[4:6]:
+        copy.wait()
+
+    def first(x, packs):
+        ystage[0, 0, pl.ds(x, 1), :] = perm[1, x, 0:1, :]
+        ystage[0, 1, pl.ds(x, 1), :] = perm[1, x, dy - 1 : dy, :]
+        return pack_into(packs, x, perm[2, x])
+
+    packs = planes(first, zero_packs)
+    for side, p in enumerate(packs):
+        zstage[0, side] = p
+    each(sends[1] + sends[2], start)
+    pending += sends[0] + sends[1] + sends[2]
 
     shift_z, shift_c = dz.bit_length() - 1, column.bit_length() - 1
     own_rows = one_hot(cell >> shift_z, dx, F32)
@@ -231,24 +243,20 @@
     near = scattered(weight, own_x3[...], own_z[...])
 
     def inner(x, carry):
-        @pl.when(x < dx - 1)
-        def _():
-            tx[x + 1] = harmonic(perm[0, x], perm[0, x + 1])
-
+        tx[x + 1] = harmonic(perm[0, x], perm[0, jnp.minimum(x + 1, dx - 1)])
         k = perm[1, x]
         ty[x] = jnp.where(row == dy - 1, 0.0, harmonic(k, pltpu.roll(k, dy - 1, 0)))
         k = perm[2, x]
         tz[x] = jnp.where(lane == dz - 1, 0.0, harmonic(k, pltpu.roll(k, dz - 1, 1)))
         return carry
 
-    lax.fori_loop(0, dx, inner, 0)
-
-    each(receives, lambda copy: copy.wait_recv())
-    for copy in loads[5:]:
-        copy.wait()
-    tx[0] = harmonic(perm[0, 0], xland[0, 0])
-    tx[dx] = harmonic(perm[0, dx - 1], xland[0, 1])
-    up_rows = []
+    loads[6].wait()
+    planes(inner, 0)
+
+    def arrived(copy):
+        copy.wait_recv()
+
+    each(list_receives, arrived)
     far = 0.0
     for other in range(nz):
         up_cell = listland[other, 0:1, :].astype(jnp.int32)
@@ -259,6 +267,11 @@
         up_z[other] = one_hot(up_cell & (dz - 1), dz, F32)
         up_own[other] = one_hot((up_remote & (column - 1)) - l * dz, dz, BF16)
         far = far + scattered(up_weight, up_x3[other], up_own[other])
+    each(receives[0] + receives[1] + receives[2], arrived)
+    for copy in loads[7:]:
+        copy.wait()
+    tx[0] = harmonic(perm[0, 0], xland[0, 0])
+    tx[dx] = harmonic(perm[0, dx - 1], xland[0, 1])
     for side, extra in ((0, near), (1, far)):
         value = 0.0
         for other in range(nz):
@@ -297,7 +310,7 @@
         value = inverse * rhs[x]
         inv[x] = inverse
         g[x] = value
-        value = value / theta
+        value = value * (1.0 / theta)
         c0[x + 1] = value
         put_rows(ystage.at[1], x, value)
         put_rows(yinv, x, inverse)
@@ -314,15 +327,13 @@
         tx[edge] = jnp.zeros((dy, dz), F32)
 
     square = dz - 2 * dx
+    sends, receives = copies(1, (xstage.at[1, 0], xstage.at[1, 1]))
+    each(sends[1] + sends[2] + sends[0], start)
+    pending += sends[0] + sends[1] + sends[2]
     now, before = c0, c1
     rho = 1.0 / sigma
     b = 0.0
     for e in range(1, SWEEPS):
-        each(pending, lambda copy: copy.wait_send())
-        sends, receives = copies(e, (xstage.at[e, 0], xstage.at[e, 1]))
-        each(sends, lambda copy: copy.start())
-        pending = sends
-
         rho_next = 1.0 / (2.0 * sigma - rho)
         a, b_old, b = rho_next * rho, b, 2.0 * rho_next / delta
         rho = rho_next
@@ -357,7 +368,7 @@
         for x in range(dx - UNROLL, dx):
             packs = bulk(x, packs, x < dx - 2)
 
-        each(receives, lambda copy: copy.wait_recv())
+        each(receives[1], arrived)
         flux = 0.0
         far = 0.0
         sides = [0.0, 0.0]
@@ -370,6 +381,7 @@
                 sides[side] = jnp.where(l == other, yland[e, side, other], sides[side])
         near = scattered(weight * flux, own_x3[...], own_z[...])
         yvalues = [hyt[0] * sides[0] + near, hyt[1] * sides[1] + far]
+        each(receives[2] + receives[0], arrived)
         for side in range(2):
             hy[side] = yvalues[side]
             hx[side] = hxt[side] * xland[e, side]
@@ -377,10 +389,10 @@
         for side in range(len(z_sides)):
             hz[side] = zvalues[side]
 
-        ends = []
-        for side, x in ((0, 0), (1, dx - 1)):
-            ends.append(before[x + 1] + b * inv[x] * (hx[side] + rims(x, zvalues)))
         if e == SWEEPS - 1:
+            ends = []
+            for side, x in ((0, 0), (1, dx - 1)):
+                ends.append(before[x + 1] + b * inv[x] * (hx[side] + rims(x, zvalues)))
             out[0] = ends[0]
             out[dx - 1] = ends[1]
 
@@ -391,8 +403,8 @@
 
             lax.fori_loop(1, dx - 1, last, 0)
             continue
-        xstage[e + 1, 0] = ends[0]
-        xstage[e + 1, 1] = ends[1]
+        sends, receives = copies(e + 1, (xstage.at[e + 1, 0], xstage.at[e + 1, 1]))
+        pending += sends[0] + sends[1] + sends[2]
         xrow = lax.broadcasted_iota(jnp.int32, (dx, dz), 0)
         xlane = lax.broadcasted_iota(jnp.int32, (dx, dz), 1)
         turned = [
@@ -407,6 +419,7 @@
                 shifted = pltpu.roll(t, lax.rem(edge + dz - y, dz), 1)
                 term = term + jnp.where(xlane == edge, shifted, 0.0)
             ystage[e + 1, side] = ypart[side] + b * yinv[side] * term
+        each(sends[1], start)
         turn[...] = jnp.concatenate(yvalues + [jnp.zeros((square, dz), F32)], axis=0).T
         for (edge, _, _, zside), p in zip(z_sides, packs):
             line = turn[pl.ds(edge, 1), :]
@@ -419,6 +432,13 @@
                 shifted = pltpu.roll(hx[side], pack_shift(x, edge), 1)
                 term = term + jnp.where(lane == x, shifted, 0.0)
             zstage[e + 1, zside] = p + b * zinv[zside] * term
+        each(sends[2], start)
+        ends = []
+        for side, x in ((0, 0), (1, dx - 1)):
+            ends.append(before[x + 1] + b * inv[x] * (hx[side] + rims(x, zvalues)))
+        xstage[e + 1, 0] = ends[0]
+        xstage[e + 1, 1] = ends[1]
+        each(sends[0], start)
         now, before = before, now
     each(pending, lambda copy: copy.wait_send())
 
@@ -437,7 +457,7 @@
     scratch = [
         V(plane, F32), V(plane, F32), V((3, *plane), F32),
         V((1, slots), jnp.int32), V((1, slots), jnp.int32), V((1, slots), jnp.int32),
-        V((1, slots), F32), dma((7,)),
+        V((1, slots), F32), dma((9,)),
         V((dx + 2, dy, dz), F32), V((dx + 2, dy, dz), F32),
         V(plane, F32), V(plane, F32),
         V((dx + 1, dy, dz), F32), V(plane, F32), V(plane, F32),

time: 39.7 us -> 38.6 us (0.972); the launches traced: 39.4 us -> 37.9 us
  Pallas kernels: 32.4 us -> 30.9 us
    pallas_call x1, Pallas kernels: 32.4 us -> 30.9 us  [local(): pl.pallas_call(functools.partial(kernel, sizes), out_shape=jax.ShapeDtype...]
where the time goes in v2:
time: 38.6 us; the launch traced here: 37.9 us
  Pallas kernels  30.9 us (80%)
  local copies, waits for them, and re-layouts  7.01 us (18%)
    pallas_call x1, Pallas kernels, local(): pl.pallas_call(functools.partial(kernel, sizes), out_shape=jax.ShapeDtype...  30.9 us
    unnamed x15, local copies, waits for them, and re-layouts  7.01 us

profile of v2, /device:TPU:0, one launch (start us, length us, event | category | flops | bytes accessed | tf_op | source)
XLA Modules:
  0.0 37.9 jit_solution(5200212891383886565)
XLA Ops:
  0.0 0.0 copy-start
  0.0 1.4 %copy-done = f32[3,32,32,128]{3,2,1,0:T(8,128)S(1)} copy-done((f32[3,32,32,128]{3,2,1,0:T(8,128)S(1)}, f32[3,32,32,128]{3,2,1,0:T(8,128)}, u32[]{:S(2)}) %copy-start) | copy-done | bytes 1572888
  1.4 0.0 copy-start.1
  1.4 1.0 %copy-done.1 = f32[32,32,128]{2,1,0:T(8,128)S(1)} copy-done((f32[32,32,128]{2,1,0:T(8,128)S(1)}, f32[32,32,128]{2,1,0:T(8,128)}, u32[]{:S(2)}) %copy-start.1) | copy-done | bytes 524312
  2.5 0.0 copy-start.2
  2.5 1.0 %copy-done.2 = f32[32,32,128]{2,1,0:T(8,128)S(1)} copy-done((f32[32,32,128]{2,1,0:T(8,128)S(1)}, f32[32,32,128]{2,1,0:T(8,128)}, u32[]{:S(2)}) %copy-start.2) | copy-done | bytes 524312
  3.5 0.0 copy-start.3
  3.5 0.7 %copy-done.3 = s32[1,1,1,512]{3,2,1,0:T(1,128)S(1)} copy-done((s32[1,1,1,512]{3,2,1,0:T(1,128)S(1)}, s32[1,1,1,512]{3,2,1,0:T(1,128)}, u32[]{:S(2)}) %copy-start.3) | copy-done | bytes 2072
  4.2 0.0 copy-start.4
  4.2 0.7 %copy-done.4 = s32[1,1,1,512]{3,2,1,0:T(1,128)S(1)} copy-done((s32[1,1,1,512]{3,2,1,0:T(1,128)S(1)}, s32[1,1,1,512]{3,2,1,0:T(1,128)}, u32[]{:S(2)}) %copy-start.4) | copy-done | bytes 2072
  4.9 0.0 copy-start.5
  4.9 0.7 %copy-done.5 = s32[1,1,1,512]{3,2,1,0:T(1,128)S(1)} copy-done((s32[1,1,1,512]{3,2,1,0:T(1,128)S(1)}, s32[1,1,1,512]{3,2,1,0:T(1,128)}, u32[]{:S(2)}) %copy-start.5) | copy-done | bytes 2072
  5.5 0.0 copy-start.6
  5.5 0.7 %copy-done.6 = f32[1,1,1,512]{3,2,1,0:T(1,128)S(1)} copy-done((f32[1,1,1,512]{3,2,1,0:T(1,128)S(1)}, f32[1,1,1,512]{3,2,1,0:T(1,128)}, u32[]{:S(2)}) %copy-start.6) | copy-done | bytes 2072
  6.2 30.9 %shard_map.73 = f32[32,32,128]{2,1,0:T(8,128)S(1)} custom-call(f32[32,32,128]{2,1,0:T(8,128)S(1)} %copy-done.1, f32[32,32,128]{2,1,0:T(8,128)S(1)} %copy-done.2, f32[3,32,32,128]{3,2,1,0:T(8,128)S(1)} %copy-done, s32[1,512]{1,0:T(1,128)S(1)} %bitcast.4, s32[1,512]{1,0:T(1,128)S(1)} %bitcast.5, s32[1,512]{1,0:T(1,128)S(1)} %bitcast.6, f32[1,512]{1,0:T(1,128)S(1)} %bitcast.7), custom_call_target="tpu_custom_call" | custom-call | tf_op jit(solution)/shard_map/pallas_call | solution.py:479
  37.1 0.8 %copy.9 = f32[32,32,128]{2,1,0:T(8,128)} copy(f32[32,32,128]{2,1,0:T(8,128)S(1)} %shard_map.73) | data formatting | bytes 1048576
Async XLA Ops:
  0.0 1.4 %copy-start = (f32[3,32,32,128]{3,2,1,0:T(8,128)S(1)}, f32[3,32,32,128]{3,2,1,0:T(8,128)}, u32[]{:S(2)}) copy-start(f32[3,32,32,128]{3,2,1,0:T(8,128)} %perm_in.1) | copy-start | bytes 4718596
  1.4 1.0 %copy-start.1 = (f32[32,32,128]{2,1,0:T(8,128)S(1)}, f32[32,32,128]{2,1,0:T(8,128)}, u32[]{:S(2)}) copy-start(f32[32,32,128]{2,1,0:T(8,128)} %rhs_in.1) | copy-start | bytes 1572868
  2.5 1.0 %copy-start.2 = (f32[32,32,128]{2,1,0:T(8,128)S(1)}, f32[32,32,128]{2,1,0:T(8,128)}, u32[]{:S(2)}) copy-start(f32[32,32,128]{2,1,0:T(8,128)} %acc_in.1) | copy-start | bytes 1572868
  3.5 0.7 %copy-start.3 = (s32[1,1,1,512]{3,2,1,0:T(1,128)S(1)}, s32[1,1,1,512]{3,2,1,0:T(1,128)}, u32[]{:S(2)}) copy-start(s32[1,1,1,512]{3,2,1,0:T(1,128)} %param.10) | copy-start | bytes 6148
  4.2 0.7 %copy-start.4 = (s32[1,1,1,512]{3,2,1,0:T(1,128)S(1)}, s32[1,1,1,512]{3,2,1,0:T(1,128)}, u32[]{:S(2)}) copy-start(s32[1,1,1,512]{3,2,1,0:T(1,128)} %param.11) | copy-start | bytes 6148
  4.9 0.7 %copy-start.5 = (s32[1,1,1,512]{3,2,1,0:T(1,128)S(1)}, s32[1,1,1,512]{3,2,1,0:T(1,128)}, u32[]{:S(2)}) copy-start(s32[1,1,1,512]{3,2,1,0:T(1,128)} %param.12) | copy-start | bytes 6148
  5.5 0.7 %copy-start.6 = (f32[1,1,1,512]{3,2,1,0:T(1,128)S(1)}, f32[1,1,1,512]{3,2,1,0:T(1,128)}, u32[]{:S(2)}) copy-start(f32[1,1,1,512]{3,2,1,0:T(1,128)} %param.13) | copy-start | bytes 6148
